TPU v7x, 32 devices: a whole 2x2x4 slice. The times are simulated.
32 devices in a mesh: seq: 8 (over y, x, core), heads: 4 (over z).
Axes of the slice: x: 2, y: 2, z: 4, core: 2. Of those that a mesh axis runs over, the one named last changes fastest.
Arguments:
- hidden_in: bfloat16 [2048, 8192], P('seq', 'heads'), may hold values from -6 to 6
- queries: bfloat16 [2048, 8192], P('seq', 'heads'), as said below
- image_kv: bfloat16 [8, 2, 6528, 1024], P('seq', None, None, 'heads'), as said below
- out_weight: bfloat16 [8192, 8192], P('seq', 'heads'), may hold values from -0.0625 to 0.0625
- gate: float32 [1], replicated, may hold values from 0.4 to 1.2
- tile_counts: int32 [8], replicated, may hold values from 1 to 4, as said below
- owners: int32 [128], replicated, may hold values from 0 to 7, as said below
- starts: int32 [128], replicated, may hold values from 0 to 3, as said below
- norm_gain: float32 [8192], P('heads'), may hold values from 0.1 to 1.9
- norm_grad: bfloat16 [2048, 8192], P('seq', 'heads'), may hold values from -6 to 6
- stream_grad: bfloat16 [2048, 8192], P('seq', 'heads'), may hold values from -6 to 6
Outputs:
- hidden_out: bfloat16 [2048, 8192], P('seq', 'heads')
- stream_in_grad: float32 [2048, 8192], P('seq', 'heads')
Inputs may be any that keep to these rules, and one draw needn't show every extreme that they name: `tile_counts`: tiles of each image; some image has 4 tiles in every draw. `owners`: the image (named by the seq index that owns it) that a block of 16 text rows attends to; of the 16 blocks of one seq index at most 2 name the same image, and in every draw some image is named by exactly 2 blocks of every seq index. `starts`: the first tile a block sees, below the tile count of the block's image; in every draw some block starts at tile 0 and some at tile 4 - 1. `image_kv`: keys and values are real-valued. real-valued queries.
All inputs are finite; a program needn't handle non-finite values.
Results may differ from a plain program's by a relative error of at most 0.007.
Values may be sent and summed in bfloat16 or wider, within the bound.
A program may use at most 128 MiB of HBM per device.

v0:
```python
import math

import jax
import jax.numpy as jnp
from jax import lax
from jax.sharding import PartitionSpec as P

D = 8192
HEAD_DIM = 128
TILE_TOK = 1601
BLOCKS_DEV = 16
CAP = 2
BLK = 16


EPS = 1e-05


def head_scores(query_head, key_block, scale):
    return (
        lax.dot_general(
            query_head, key_block, (((1,), (1,)), ((), ())), preferred_element_type=jnp.float32
        )
        * scale
    )


def local(
    hidden_in,
    queries,
    image_kv,
    out_weight,
    gate,
    tile_counts,
    owners,
    starts,
    norm_gain,
    norm_grad,
    stream_grad,
):
    seq_count = lax.axis_size("seq")
    here = lax.axis_index("seq")
    tok_rows, q_width = queries.shape
    q_heads = q_width // HEAD_DIM
    kv_width = image_kv.shape[3]
    group = q_heads // (kv_width // HEAD_DIM)
    slot_count = seq_count * CAP
    scale = 1.0 / math.sqrt(HEAD_DIM)
    owner_table = owners.reshape(seq_count, BLOCKS_DEV)
    start_table = starts.reshape(seq_count, BLOCKS_DEV)
    my_owner = lax.dynamic_index_in_dim(owner_table, here, 0, keepdims=False)
    block_ids = jnp.arange(BLOCKS_DEV)
    same = my_owner[:, None] == my_owner[None, :]
    earlier = block_ids[None, :] < block_ids[:, None]
    my_rank = jnp.sum(jnp.logical_and(same, earlier).astype(jnp.int32), axis=1)
    my_slot = my_owner * CAP + my_rank
    placing = (my_slot[:, None] == jnp.arange(slot_count)[None, :]).astype(jnp.bfloat16)
    q_blocks = queries.reshape(BLOCKS_DEV, BLK, q_width)
    outgoing = jnp.einsum(
        "bs,brc->src", placing, q_blocks, preferred_element_type=jnp.float32
    ).astype(jnp.bfloat16)
    outgoing = outgoing.reshape(seq_count, CAP, BLK, q_width)
    arriving = owner_table == here
    arrive_rank = jnp.cumsum(arriving.astype(jnp.int32), axis=1) - 1
    slot_hit = jnp.logical_and(
        arriving[:, :, None], arrive_rank[:, :, None] == jnp.arange(CAP)[None, None, :]
    )
    slot_start = jnp.sum(jnp.where(slot_hit, start_table[:, :, None], 0), axis=1)
    tile_here = lax.dynamic_index_in_dim(tile_counts, here, 0, keepdims=False)
    key_end = tile_here * TILE_TOK
    keys_here = image_kv[0, 0]
    values_here = image_kv[0, 1]
    received = lax.all_to_all(outgoing, "seq", split_axis=0, concat_axis=0, tiled=True)
    flat = received.reshape(-1, q_width)
    row_first = jnp.broadcast_to(slot_start[:, :, None], received.shape[:3]).reshape(-1) * TILE_TOK

    def one_head(head):
        query_head = lax.dynamic_slice_in_dim(flat, head * HEAD_DIM, HEAD_DIM, 1)
        key_column = head // group * HEAD_DIM
        key_head = lax.dynamic_slice_in_dim(keys_here, key_column, HEAD_DIM, 1)
        value_head = lax.dynamic_slice_in_dim(values_here, key_column, HEAD_DIM, 1)
        spot = jnp.arange(key_head.shape[0])
        seen = jnp.logical_and(spot[None, :] >= row_first[:, None], spot[None, :] < key_end)
        scores = jnp.where(seen, head_scores(query_head, key_head, scale), -jnp.inf)
        highest = jnp.max(scores, axis=1, keepdims=True)
        probs = jnp.exp(scores - highest)
        total = jnp.sum(probs, axis=1, keepdims=True)
        mixed = jnp.dot(probs.astype(jnp.bfloat16), value_head, preferred_element_type=jnp.float32)
        return (mixed / total).astype(jnp.bfloat16)

    heads_out = lax.map(one_head, jnp.arange(q_heads))
    merged = jnp.moveaxis(heads_out, 0, 1).reshape(received.shape)
    returned = lax.all_to_all(merged, "seq", split_axis=0, concat_axis=0, tiled=True)
    context = jnp.einsum(
        "bs,src->brc",
        placing,
        returned.reshape(slot_count, BLK, q_width),
        preferred_element_type=jnp.float32,
    )
    context = context.astype(jnp.bfloat16).reshape(tok_rows, q_width)
    full_context = lax.all_gather(context, "heads", axis=1, tiled=True)
    feature_rows = lax.all_to_all(full_context, "seq", split_axis=1, concat_axis=0, tiled=True)
    branch = lax.psum_scatter(
        jnp.dot(feature_rows, out_weight, preferred_element_type=jnp.float32).astype(jnp.bfloat16),
        "seq",
        scatter_dimension=0,
        tiled=True,
    ).astype(jnp.float32)
    hidden_out = (hidden_in.astype(jnp.float32) + jnp.tanh(gate[0]) * branch).astype(jnp.bfloat16)
    hidden = hidden_out.astype(jnp.float32)
    scaled = norm_gain[None, :] * norm_grad.astype(jnp.float32)
    squares, product = lax.psum(
        (jnp.sum(hidden * hidden, axis=1), jnp.sum(hidden * scaled, axis=1)), "heads"
    )
    inverse = lax.rsqrt(squares / D + EPS)[:, None]
    project = (product / D)[:, None]
    stream_in_grad = (
        stream_grad.astype(jnp.float32) + inverse * scaled - inverse**3 * project * hidden
    )
    return (hidden_out, stream_in_grad)


def solution(mesh):
    placed = (
        P("seq", "heads"),
        P("seq", "heads"),
        P("seq", None, None, "heads"),
        P("seq", "heads"),
        P(),
        P(),
        P(),
        P(),
        P("heads"),
        P("seq", "heads"),
        P("seq", "heads"),
    )
    return jax.shard_map(
        local,
        mesh=mesh,
        in_specs=placed,
        out_specs=(P("seq", "heads"), P("seq", "heads")),
        check_vma=False,
    )
```

profile of v0, /device:TPU:0, one launch (start us, length us, event | category | flops | bytes accessed | tf_op | source)
XLA Modules:
  0.0 481.5 jit_solution(16272396503835100332)
XLA Ops:
  12.3 5.2 %all-to-all-start = ((bf16[8,2,16,2048]{3,1,2,0:T(2,128)(2,1)}), bf16[8,2,16,2048]{3,1,2,0:T(2,128)(2,1)S(1)}, u32[]{:S(2)}, u32[]{:S(2)}) async-start(bf16[8,2,16,2048]{3,1,2,0:T(2,128)(2,1)} %copy.44), calls=%async_computation | async-start | bytes 2097152 | tf_op jit(solution)/shard_map/all_to_all | solution.py:73
  17.5 6.2 %slice_bitcast_fusion = (bf16[6528,256]{1,0:T(8,128)(2,1)}, bf16[6528,256]{1,0:T(8,128)(2,1)}) fusion(bf16[1,2,6528,256]{3,2,1,0:T(8,128)(2,1)} %param.15), kind=kLoop, calls=%fused_computation.22 | loop fusion | bytes 13369344 | tf_op jit(solution)/shard_map/squeeze | solution.py:72
  25.5 7.4 %all-to-all-done = bf16[8,2,16,2048]{3,1,2,0:T(2,128)(2,1)S(1)} async-done(((bf16[8,2,16,2048]{3,1,2,0:T(2,128)(2,1)}), bf16[8,2,16,2048]{3,1,2,0:T(2,128)(2,1)S(1)}, u32[]{:S(2)}, u32[]{:S(2)}) %all-to-all-start) | async-done | bytes 1048608 | tf_op jit(solution)/shard_map/all_to_all | solution.py:73
  33.3 186.2 %while.13 = (s32[]{:T(128)}, bf16[16,256,128]{2,1,0:T(8,128)(2,1)}, s32[]{:T(128)}, s32[16]{0:T(128)S(1)}, bf16[256,2048]{1,0:T(8,128)(2,1)S(1)}, /*index=5*/bf1...) while((s32[]{:T(128)}, bf16[16,256,128]{2,1,0:T(8,128)(2,1)}, ...), condition=%wide.region_6.7_spmd.clone, body=%wide.region_3.6_spmd.clone.sunk | while | flops 870750080 | bytes 36920704 | solution.py:91
  37.3 3.7 fusion.58
  48.9 3.7 fusion.58
  60.6 3.7 fusion.58
  72.2 3.7 fusion.58
  83.9 3.7 fusion.58
  95.5 3.7 fusion.58
  107.1 3.7 fusion.58
  118.8 3.7 fusion.58
  153.7 3.7 fusion.58
  165.3 3.7 fusion.58
  177.0 3.7 fusion.58
  188.6 3.7 fusion.58
  200.2 3.7 fusion.58
  211.9 3.7 fusion.58
  221.9 17.8 %all_to_all.29 = bf16[8,2,16,2048]{3,2,1,0:T(8,128)(2,1)S(1)} all-to-all(bf16[8,2,16,2048]{3,2,1,0:T(8,128)(2,1)S(1)} %reshape.81), channel_id=1, replica_groups=mesh['seq'=8,'heads'=4] {'seq'}, dimensions={0} | all-to-all | bytes 2097152 | tf_op jit(solution)/shard_map/all_to_all | solution.py:93
  242.6 80.2 %all-gather.2.cloned.1.call-done = bf16[256,8192]{1,0:T(8,128)(2,1)} async-done(((bf16[256,2048]{1,0:T(8,128)(2,1)}), bf16[256,8192]{1,0:T(8,128)(2,1)}) %all-gather.2.cloned.1.call-update) | async-done | bytes 4194320 | tf_op jit(solution)/shard_map/all_gather | solution.py:101
  325.5 53.0 %all_to_all.30 = bf16[256,8,1024]{2,0,1:T(8,128)(2,1)S(1)} all-to-all(bf16[256,8,1024]{2,0,1:T(8,128)(2,1)S(1)} %bitcast.41), channel_id=1, replica_groups=mesh['seq'=8,'heads'=4] {'seq'}, dimensions={1} | all-to-all | bytes 8388608 | tf_op jit(solution)/shard_map/all_to_all | solution.py:102
  378.4 10.9 %convolution_convert_fusion = bf16[2048,2048]{1,0:T(8,128)(2,1)} fusion(bf16[2048,1024]{1,0:T(8,128)(2,1)S(1)} %bitcast.44, bf16[1024,2048]{1,0:T(8,128)(2,1)S(1)} %copy-done.6), kind=kOutput, calls=%fused_computation.20 | convolution fusion | flops 8594128896 | bytes 16777216 | tf_op jit(solution)/shard_map/dot_general | solution.py:104
  390.1 67.4 %reduce-scatter.2.cloned.1.call-done = bf16[256,2048]{1,0:T(8,128)(2,1)} async-done(((bf16[2048,2048]{1,0:T(8,128)(2,1)}), bf16[256,2048]{1,0:T(8,128)(2,1)}) %reduce-scatter.2.cloned.1.call-update) | async-done | bytes 1048592 | tf_op jit(solution)/shard_map/reduce_scatter | solution.py:103
  459.8 11.7 %all-reduce = (f32[256]{0:T(256)S(1)}, f32[256]{0:T(256)S(1)}) all-reduce(f32[256]{0:T(256)S(1)} %get-tuple-element.133, f32[256]{0:T(256)S(1)} %get-tuple-element.132), channel_id=1, replica_groups=mesh['seq'=8,'heads'=4] {'heads'}, use_global_device_ids=true, to_apply=%region_11.12 | all-reduce | flops 512 | bytes 4096 | tf_op jit(solution)/shard_map/psum | solution.py:112
  (174 shorter events, 101.9 us)
Async XLA Ops:
  12.3 20.6 %all-to-all-start = ((bf16[8,2,16,2048]{3,1,2,0:T(2,128)(2,1)}), bf16[8,2,16,2048]{3,1,2,0:T(2,128)(2,1)S(1)}, u32[]{:S(2)}, u32[]{:S(2)}) async-start(bf16[8,2,16,2048]{3,1,2,0:T(2,128)(2,1)} %copy.44), calls=%async_computation | async-start | bytes 2097152 | tf_op jit(solution)/shard_map/all_to_all | solution.py:73
  17.5 6.4 %copy-start.5 = (s32[128]{0:T(128)S(1)}, s32[128]{0:T(128)}, u32[]{:S(2)}) copy-start(s32[128]{0:T(128)} %param.20) | copy-start | bytes 1540
  17.5 6.7 %copy-start.7 = (s32[8]{0:T(128)S(1)}, s32[8]{0:T(128)}, u32[]{:S(2)}) copy-start(s32[8]{0:T(128)} %param.18) | copy-start | bytes 100
  17.5 305.3 %all-gather.2.cloned.1.call-start = ((), (), s32[]{:S(2)}) async-start(), calls=%async_computation.4 | async-start | bytes 5242880 | tf_op jit(solution)/shard_map/all_gather | solution.py:101
  41.0 2.0 copy-start.1
  52.7 2.0 copy-start.1
  75.9 2.0 copy-start.1
  87.6 2.0 copy-start.1
  99.2 2.0 copy-start.1
  110.8 2.0 copy-start.1
  122.5 2.0 copy-start.1
  134.1 2.0 copy-start.1
  145.8 2.0 copy-start.1
  157.4 2.0 copy-start.1
  169.0 2.0 copy-start.1
  180.7 2.0 copy-start.1
  192.3 2.0 copy-start.1
  204.0 2.0 copy-start.1
  215.6 2.0 copy-start.1
  242.6 214.9 %reduce-scatter.2.cloned.1.call-start = ((), (), s32[]{:S(2)}) async-start(), calls=%async_computation.5 | async-start | bytes 9437184 | tf_op jit(solution)/shard_map/reduce_scatter | solution.py:103
  325.5 53.0 %copy-start.6 = (bf16[1024,2048]{1,0:T(8,128)(2,1)S(1)}, bf16[1024,2048]{1,0:T(8,128)(2,1)}, u32[]{:S(2)}) copy-start(bf16[1024,2048]{1,0:T(8,128)(2,1)} %param.16) | copy-start | bytes 12582916
  389.3 68.2 %copy-start.2 = (bf16[256,2048]{1,0:T(8,128)(2,1)S(1)}, bf16[256,2048]{1,0:T(8,128)(2,1)}, u32[]{:S(2)}) copy-start(bf16[256,2048]{1,0:T(8,128)(2,1)} %param.22) | copy-start | bytes 3145732
  389.3 68.2 %copy-start.4 = (f32[2048]{0:T(1024)S(1)}, f32[2048]{0:T(1024)}, u32[]{:S(2)}) copy-start(f32[2048]{0:T(1024)} %param.21) | copy-start | bytes 24580
  459.8 14.9 %copy-start.3 = (bf16[256,2048]{1,0:T(8,128)(2,1)}, bf16[256,2048]{1,0:T(8,128)(2,1)S(1)}, u32[]{:S(2)}) copy-start(bf16[256,2048]{1,0:T(8,128)(2,1)S(1)} %get-tuple-element.152) | copy-start | bytes 3145732
  (2 other events, 3.2 us)
Sparse Core Ops, SparseCore 0:
  242.7 80.1 all-gather.1
  389.5 67.9 reduce-scatter.1
where the time goes:
time: 484 us; the launch traced here: 482 us
  waiting for transfers between devices  155 us (32%)
  matrix products  104 us (21%)
  blocking collectives  82.4 us (17%)
  loops' own time  52.4 us (11%)
  local copies, waits for them, and re-layouts  43.2 us (9%)
  other arithmetic  23.5 us (5%)
  between operations  15.6 us (3%)
  starting transfers between devices  5.25 us (1%)
    all_gather x1, waiting for transfers between devices, local(): full_context = lax.all_gather(context, 'heads', axis=1, tiled=True)  80.2 us
    reduce_scatter x1, waiting for transfers between devices, local(): lax.psum_scatter(jnp.dot(feature_rows, out_weight, preferred_element_type...  67.4 us
    dot_general x16, matrix products, head_scores(): lax.dot_general(query_head, key_block, (((1,), (1,)), ((), ())), preferre...  59.4 us
    all_to_all x1, blocking collectives, local(): lax.all_to_all(full_context, 'seq', split_axis=1, concat_axis=0, tiled=True)  53 us
    another operation x1, loops' own time, local(): heads_out = lax.map(one_head, jnp.arange(q_heads))  52.4 us
    dot_general x16, matrix products, one_head(): jnp.dot(probs.astype(jnp.bfloat16), value_head, preferred_element_type=jn...  31.3 us
    all_to_all x1, blocking collectives, local(): lax.all_to_all(merged, 'seq', split_axis=0, concat_axis=0, tiled=True)  17.8 us
    reduce_sum x16, other arithmetic, one_head(): total = jnp.sum(probs, axis=1, keepdims=True)  17.3 us
  transfers between devices with their start and end apart: 3, of which 3 were waited for; matrix products, arithmetic and copies ran while one was open for 2% of the time, Pallas kernels for 0%

commit v1 on v0

v1 whole, which is shorter than its diff:
```python
import math

import jax
import jax.numpy as jnp
from jax import lax
from jax.experimental import pallas as pl
from jax.experimental.pallas import tpu as pltpu
from jax.sharding import PartitionSpec as P

D = 8192
HEAD_DIM = 128
TILE_TOK = 1601
BLOCKS_DEV = 16
CAP = 2
BLK = 16


EPS = 1e-05


KEY_BLOCK = 1792
KEY_PART = 256
LANES = 128
GROUP_SLOTS = 4


def attend_body(order_ref, first_ref, tiles_ref, q_ref, k_ref, v_ref, o_ref, qs, vx, acc, top):
    step = pl.program_id(0)
    heads = q_ref.shape[1] // HEAD_DIM
    per_head = GROUP_SLOTS * BLK
    rows = heads * per_head
    factor = math.log2(math.e) / math.sqrt(HEAD_DIM)

    @pl.when(step == 0)
    def _():
        vx[:, :HEAD_DIM] = v_ref[0, 0]
        vx[:, HEAD_DIM:] = jnp.ones((vx.shape[0], HEAD_DIM), jnp.bfloat16)

    for slot in range(GROUP_SLOTS):
        place = order_ref[step * GROUP_SLOTS + slot]
        source = q_ref[pl.ds(pl.multiple_of(place * BLK, BLK), BLK), :]
        for head in range(heads):
            qs[pl.ds(head * per_head + slot * BLK, BLK), :] = source[
                :, head * HEAD_DIM : (head + 1) * HEAD_DIM
            ]
    acc[...] = jnp.zeros_like(acc)
    top[...] = jnp.full_like(top, -3e38)
    slot_of = lax.broadcasted_iota(jnp.int32, (rows, LANES), 0) % per_head // BLK
    first = jnp.zeros((rows, LANES), jnp.int32)
    lowest = first_ref[step * GROUP_SLOTS]
    for slot in range(GROUP_SLOTS):
        first = jnp.where(slot_of == slot, first_ref[step * GROUP_SLOTS + slot], first)

    @pl.loop(lowest, tiles_ref[0])
    def _(tile):
        base = pl.multiple_of(tile * TILE_TOK // LANES * LANES, LANES)
        low = tile * TILE_TOK - base
        high = low + TILE_TOK
        query = qs[...]
        parts = []
        best = None
        for part in range(KEY_BLOCK // KEY_PART):
            keys = k_ref[0, 0, pl.ds(base + part * KEY_PART, KEY_PART), :]
            scores = lax.dot_general(
                query, keys, (((1,), (1,)), ((), ())), preferred_element_type=jnp.float32
            )
            spot = lax.broadcasted_iota(jnp.int32, scores.shape, 1) + part * KEY_PART
            if part == 0:
                scores = jnp.where(spot >= low, scores, -jnp.inf)
            if (part + 1) * KEY_PART > TILE_TOK:
                scores = jnp.where(spot < high, scores, -jnp.inf)
            parts.append(scores)
            peak = jnp.maximum(scores[:, :LANES], scores[:, LANES:])
            best = peak if best is None else jnp.maximum(best, peak)
        before = top[...]
        seen = first <= tile
        highest = jnp.maximum(before, jnp.max(best, axis=1, keepdims=True))
        highest = jnp.where(seen, highest, before)
        top[...] = highest
        alpha = jnp.exp2((before - highest) * factor)
        shift = jnp.where(seen, highest * factor, jnp.inf)
        shift = jnp.concatenate([shift, shift], axis=1)
        mixed = None
        for part in range(KEY_BLOCK // KEY_PART):
            probs = jnp.exp2(parts[part] * factor - shift).astype(jnp.bfloat16)
            values = vx[pl.ds(base + part * KEY_PART, KEY_PART), :]
            term = jnp.dot(probs, values, preferred_element_type=jnp.float32)
            mixed = term if mixed is None else mixed + term
        acc[...] = acc[...] * jnp.concatenate([alpha, alpha], axis=1) + mixed

    result = (acc[:, :HEAD_DIM] / acc[:, HEAD_DIM:]).astype(jnp.bfloat16)
    for slot in range(GROUP_SLOTS):
        place = order_ref[step * GROUP_SLOTS + slot]
        for head in range(heads):
            start = head * per_head + slot * BLK
            o_ref[
                pl.ds(pl.multiple_of(place * BLK, BLK), BLK),
                head * HEAD_DIM : (head + 1) * HEAD_DIM,
            ] = result[start : start + BLK]


def attend(order, first, tiles, flat, image_kv, index, width, kv_head):
    rows = flat.shape[0]
    keys = image_kv.shape[2]
    stacked = width // HEAD_DIM * GROUP_SLOTS * BLK
    return pl.pallas_call(
        attend_body,
        grid_spec=pltpu.PrefetchScalarGridSpec(
            num_scalar_prefetch=3,
            grid=(rows // (GROUP_SLOTS * BLK),),
            in_specs=[
                pl.BlockSpec((rows, width), lambda g, *_: (0, index)),
                pl.BlockSpec((1, 1, keys, HEAD_DIM), lambda g, *_: (0, 0, 0, kv_head)),
                pl.BlockSpec((1, 1, keys, HEAD_DIM), lambda g, *_: (0, 1, 0, kv_head)),
            ],
            out_specs=pl.BlockSpec((rows, width), lambda g, *_: (0, 0)),
            scratch_shapes=[
                pltpu.VMEM((stacked, HEAD_DIM), jnp.bfloat16),
                pltpu.VMEM((keys, 2 * HEAD_DIM), jnp.bfloat16),
                pltpu.VMEM((stacked, 2 * HEAD_DIM), jnp.float32),
                pltpu.VMEM((stacked, LANES), jnp.float32),
            ],
        ),
        out_shape=jax.ShapeDtypeStruct((rows, width), jnp.bfloat16),
        compiler_params=pltpu.CompilerParams(vmem_limit_bytes=40 * 2**20),
        cost_estimate=pl.CostEstimate(
            flops=4 * rows * width * keys,
            bytes_accessed=4 * keys * HEAD_DIM + 4 * rows * width,
            transcendentals=rows * width // HEAD_DIM * keys,
        ),
    )(order, first, tiles, flat, image_kv, image_kv)


def local(
    hidden_in,
    queries,
    image_kv,
    out_weight,
    gate,
    tile_counts,
    owners,
    starts,
    norm_gain,
    norm_grad,
    stream_grad,
):
    seq_count = lax.axis_size("seq")
    here = lax.axis_index("seq")
    tok_rows, q_width = queries.shape
    q_heads = q_width // HEAD_DIM
    kv_width = image_kv.shape[3]
    group = q_heads // (kv_width // HEAD_DIM)
    slot_count = seq_count * CAP
    owner_table = owners.reshape(seq_count, BLOCKS_DEV)
    start_table = starts.reshape(seq_count, BLOCKS_DEV)
    my_owner = lax.dynamic_index_in_dim(owner_table, here, 0, keepdims=False)
    block_ids = jnp.arange(BLOCKS_DEV)
    same = my_owner[:, None] == my_owner[None, :]
    earlier = block_ids[None, :] < block_ids[:, None]
    my_rank = jnp.sum(jnp.logical_and(same, earlier).astype(jnp.int32), axis=1)
    my_slot = my_owner * CAP + my_rank
    placing = (my_slot[:, None] == jnp.arange(slot_count)[None, :]).astype(jnp.bfloat16)
    q_blocks = queries.reshape(BLOCKS_DEV, BLK, q_width)
    outgoing = jnp.einsum(
        "bs,brc->src", placing, q_blocks, preferred_element_type=jnp.float32
    ).astype(jnp.bfloat16)
    outgoing = outgoing.reshape(seq_count, CAP, BLK, q_width)
    arriving = owner_table == here
    arrive_rank = jnp.cumsum(arriving.astype(jnp.int32), axis=1) - 1
    slot_hit = jnp.logical_and(
        arriving[:, :, None], arrive_rank[:, :, None] == jnp.arange(CAP)[None, None, :]
    )
    slot_start = jnp.sum(jnp.where(slot_hit, start_table[:, :, None], 0), axis=1)
    tile_here = lax.dynamic_index_in_dim(tile_counts, here, 0, keepdims=False)
    received = lax.all_to_all(outgoing, "seq", split_axis=0, concat_axis=0, tiled=True)
    flat = received.reshape(-1, q_width)
    slot_first = slot_start.reshape(-1)
    order = jnp.argsort(slot_first).astype(jnp.int32)
    sorted_first = slot_first[order]
    row_width = out_weight.shape[0]
    width = group * HEAD_DIM // 2
    pieces = row_width // width
    gathered = []
    for index in range(q_width // width):
        mixed = attend(
            order, sorted_first, tile_here[None], flat, image_kv, index, width, index // 2
        )
        gathered.append(lax.all_gather(mixed, "heads", axis=0))
    stacked = jnp.stack(gathered).reshape(-1, pieces, len(gathered[0]), flat.shape[0], width)
    outgoing = jnp.transpose(stacked, (2, 0, 3, 1, 4)).reshape(seq_count, flat.shape[0], row_width)
    feature_rows = lax.all_to_all(outgoing, "seq", split_axis=0, concat_axis=0, tiled=True)
    feature_rows = feature_rows.reshape(seq_count, seq_count, CAP * BLK, row_width)
    feature_rows = jnp.swapaxes(feature_rows, 0, 1).reshape(-1, row_width)
    slots = lax.psum_scatter(
        jnp.dot(feature_rows, out_weight, preferred_element_type=jnp.float32).astype(jnp.bfloat16),
        "seq",
        scatter_dimension=0,
        tiled=True,
    )
    branch = jnp.einsum(
        "bs,src->brc",
        placing,
        slots.reshape(slot_count, BLK, -1),
        preferred_element_type=jnp.float32,
    ).reshape(tok_rows, -1)
    hidden_out = (hidden_in.astype(jnp.float32) + jnp.tanh(gate[0]) * branch).astype(jnp.bfloat16)
    hidden = hidden_out.astype(jnp.float32)
    scaled = norm_gain[None, :] * norm_grad.astype(jnp.float32)
    squares, product = lax.psum(
        (jnp.sum(hidden * hidden, axis=1), jnp.sum(hidden * scaled, axis=1)), "heads"
    )
    inverse = lax.rsqrt(squares / D + EPS)[:, None]
    project = (product / D)[:, None]
    stream_in_grad = (
        stream_grad.astype(jnp.float32) + inverse * scaled - inverse**3 * project * hidden
    )
    return (hidden_out, stream_in_grad)


def solution(mesh):
    placed = (
        P("seq", "heads"),
        P("seq", "heads"),
        P("seq", None, None, "heads"),
        P("seq", "heads"),
        P(),
        P(),
        P(),
        P(),
        P("heads"),
        P("seq", "heads"),
        P("seq", "heads"),
    )
    return jax.shard_map(
        local,
        mesh=mesh,
        in_specs=placed,
        out_specs=(P("seq", "heads"), P("seq", "heads")),
        check_vma=False,
    )
```

time: 484 us -> 349 us (0.72)
  matrix products: 104 us -> 14.7 us
  Pallas kernels: 0 us -> 63.4 us
  loops' own time: 52.4 us -> 0 us
  blocking collectives: 82.4 us -> 65.2 us
  waiting for transfers between devices: 155 us -> 140 us
  other arithmetic: 23.5 us -> 9.33 us
  local copies, waits for them, and re-layouts: 43.2 us -> 34.5 us
    dot_general x33 -> x1, matrix products: 91.9 us -> 2.49 us  [local(): jnp.einsum('bs,src->brc', placing, slots.reshape(slot_count, BLK, -1), pr...]
    pallas_call x0 -> x4, Pallas kernels: none -> 63.4 us  [attend(): pl.pallas_call(attend_body, grid_spec=pltpu.PrefetchScalarGridSpec(num_sc...]
    another operation x1 -> x0, loops' own time: 52.4 us -> none  [local(): heads_out = lax.map(one_head, jnp.arange(q_heads))]
    all_gather x1 -> x4, waiting for transfers between devices: 80.2 us -> 59.7 us  [local(): gathered.append(lax.all_gather(mixed, 'heads', axis=0))]
    reduce_sum x16 -> x0, other arithmetic: 17.3 us -> none  [one_head(): total = jnp.sum(probs, axis=1, keepdims=True)]
    all_to_all x2 -> x1, blocking collectives: 70.7 us -> 53.5 us  [local(): lax.all_to_all(outgoing, 'seq', split_axis=0, concat_axis=0, tiled=True)]
    while x32 -> x0, local copies, waits for them, and re-layouts: 13.8 us -> none
    unnamed x15 -> x24, local copies, waits for them, and re-layouts: 0.32 us -> 12.7 us
  transfers between devices with their start and end apart: 3 -> 6, of which waited for: 3 -> 5; matrix products, arithmetic and copies ran while one was open for 2% -> 1% of each run, Pallas kernels for 0% -> 14%
where the time goes in v1:
time: 349 us; the launch traced here: 348 us
  waiting for transfers between devices  140 us (40%)
  blocking collectives  65.2 us (19%)
  Pallas kernels  63.4 us (18%)
  local copies, waits for them, and re-layouts  34.5 us (10%)
  matrix products  14.7 us (4%)
  between operations  14.6 us (4%)
  other arithmetic  9.33 us (3%)
  starting transfers between devices  5.55 us (2%)
    reduce_scatter x1, waiting for transfers between devices, local(): lax.psum_scatter(jnp.dot(feature_rows, out_weight, preferred_element_type...  68.4 us
    pallas_call x4, Pallas kernels, attend(): pl.pallas_call(attend_body, grid_spec=pltpu.PrefetchScalarGridSpec(num_sc...  63.4 us
    all_gather x4, waiting for transfers between devices, local(): gathered.append(lax.all_gather(mixed, 'heads', axis=0))  59.7 us
    all_to_all x1, blocking collectives, local(): lax.all_to_all(outgoing, 'seq', split_axis=0, concat_axis=0, tiled=True)  53.5 us
    unnamed x24, local copies, waits for them, and re-layouts  12.7 us
    all_to_all x1, waiting for transfers between devices, local(): lax.all_to_all(outgoing, 'seq', split_axis=0, concat_axis=0, tiled=True)  12.2 us
    psum x1, blocking collectives, local(): lax.psum((jnp.sum(hidden * hidden, axis=1), jnp.sum(hidden * scaled, axis...  11.7 us
    dot_general x1, matrix products, local(): jnp.dot(feature_rows, out_weight, preferred_element_type=jnp.float32)  10.9 us
  transfers between devices with their start and end apart: 6, of which 5 were waited for; matrix products, arithmetic and copies ran while one was open for 1% of the time, Pallas kernels for 14%

profile of v1, /device:TPU:0, one launch (start us, length us, event | category | flops | bytes accessed | tf_op | source)
XLA Modules:
  0.0 347.7 jit_solution(6162930551188827977)
XLA Ops:
  8.4 1.3 convolution_convert_fusion.1
  9.7 1.5 copy.43
  11.3 5.2 %all-to-all-start = ((bf16[8,2,16,2048]{3,2,1,0:T(8,128)(2,1)}), bf16[8,2,16,2048]{3,2,1,0:T(8,128)(2,1)S(1)}, u32[]{:S(2)}, u32[]{:S(2)}) async-start(bf16[8,2,16,2048]{3,2,1,0:T(8,128)(2,1)} %bitcast.5), calls=%async_computation | async-start | bytes 2097152 | tf_op jit(solution)/shard_map/all_to_all | solution.py:175
  19.7 12.2 %all-to-all-done = bf16[8,2,16,2048]{3,2,1,0:T(8,128)(2,1)S(1)} async-done(((bf16[8,2,16,2048]{3,2,1,0:T(8,128)(2,1)}), bf16[8,2,16,2048]{3,2,1,0:T(8,128)(2,1)S(1)}, u32[]{:S(2)}, u32[]{:S(2)}) %all-to-all-start) | async-done | bytes 1048608 | tf_op jit(solution)/shard_map/all_to_all | solution.py:175
  31.9 2.9 copy-done.1
  34.8 15.8 %shard_map.122 = bf16[256,512]{1,0:T(8,128)(2,1)} custom-call(s32[16]{0:T(128)S(1)} %get-tuple-element.3.order_ref, s32[16]{0:T(128)S(1)} %gather_fusion, s32[1]{0:T(128)} %dynamic_slice.9.tiles_ref, bf16[256,2048]{1,0:T(8,128)(2,1)S(1)} %bitcast.35, bf16[1,2,6528,256]{3,2,1,0:T(8,128)(2,1)S(1)} %copy-done.1, bf16[1,2,6528,256]{3,2,1,0:T(8,128)(2,1)S(1)} %copy-done.1), custom_call_target="tpu_custom_call" | custom-call | flops 3422552064 | bytes 3866624 | tf_op jit(solution)/shard_map/pallas_call | solution.py:106
  50.7 2.9 copy-done.2
  53.6 15.9 %shard_map.123 = bf16[256,512]{1,0:T(8,128)(2,1)} custom-call(s32[16]{0:T(128)S(1)} %get-tuple-element.3.order_ref, s32[16]{0:T(128)S(1)} %gather_fusion, s32[1]{0:T(128)} %dynamic_slice.9.tiles_ref, bf16[256,2048]{1,0:T(8,128)(2,1)S(1)} %bitcast.36, bf16[1,2,6528,256]{3,2,1,0:T(8,128)(2,1)S(1)} %copy-done.2, bf16[1,2,6528,256]{3,2,1,0:T(8,128)(2,1)S(1)} %copy-done.2), custom_call_target="tpu_custom_call" | custom-call | flops 3422552064 | bytes 3866624 | tf_op jit(solution)/shard_map/pallas_call | solution.py:106
  69.5 2.9 copy-done.3
  72.5 15.9 %shard_map.124 = bf16[256,512]{1,0:T(8,128)(2,1)} custom-call(s32[16]{0:T(128)S(1)} %get-tuple-element.3.order_ref, s32[16]{0:T(128)S(1)} %gather_fusion, s32[1]{0:T(128)} %dynamic_slice.9.tiles_ref, bf16[256,2048]{1,0:T(8,128)(2,1)S(1)} %bitcast.37, bf16[1,2,6528,256]{3,2,1,0:T(8,128)(2,1)S(1)} %copy-done.3, bf16[1,2,6528,256]{3,2,1,0:T(8,128)(2,1)S(1)} %copy-done.3), custom_call_target="tpu_custom_call" | custom-call | flops 3422552064 | bytes 3866624 | tf_op jit(solution)/shard_map/pallas_call | solution.py:106
  88.4 2.9 copy-done.4
  91.3 15.9 %shard_map.125 = bf16[256,512]{1,0:T(8,128)(2,1)} custom-call(s32[16]{0:T(128)S(1)} %get-tuple-element.3.order_ref, s32[16]{0:T(128)S(1)} %gather_fusion, s32[1]{0:T(128)} %dynamic_slice.9.tiles_ref, bf16[256,2048]{1,0:T(8,128)(2,1)S(1)} %bitcast.38, bf16[1,2,6528,256]{3,2,1,0:T(8,128)(2,1)S(1)} %copy-done.4, bf16[1,2,6528,256]{3,2,1,0:T(8,128)(2,1)S(1)} %copy-done.4), custom_call_target="tpu_custom_call" | custom-call | flops 3422552064 | bytes 3866624 | tf_op jit(solution)/shard_map/pallas_call | solution.py:106
  108.1 29.6 %all-gather.13.cloned.1.call-done = bf16[1024,512]{1,0:T(8,128)(2,1)} async-done(((bf16[256,512]{1,0:T(8,128)(2,1)}), bf16[1024,512]{1,0:T(8,128)(2,1)}) %all-gather.13.cloned.1.call-update) | async-done | bytes 1048592 | tf_op jit(solution)/shard_map/all_gather | solution.py:188
  137.7 29.5 %all-gather.15.cloned.1.call-done = bf16[1024,512]{1,0:T(8,128)(2,1)} async-done(((bf16[256,512]{1,0:T(8,128)(2,1)}), bf16[1024,512]{1,0:T(8,128)(2,1)}) %all-gather.15.cloned.1.call-update) | async-done | bytes 1048592 | tf_op jit(solution)/shard_map/all_gather | solution.py:188
  167.1 3.7 %pad_maximum_fusion = bf16[4,4,256,512]{3,2,1,0:T(8,128)(2,1)} fusion(bf16[1,4,256,512]{3,2,1,0:T(8,128)(2,1)} %bitcast.46, bf16[1,4,256,512]{3,2,1,0:T(8,128)(2,1)} %bitcast.45, bf16[1,4,256,512]{3,2,1,0:T(8,128)(2,1)} %bitcast.44, bf16[1,4,256,512]{3,2,1,0:T(8,128)(2,1)} %bitcast.43), kind=kLoop, calls=%fused_computation.2 | loop fusion | flops 6291456 | bytes 8388608 | tf_op jit(solution)/shard_map/stack | solution.py:189
  170.9 7.3 %copy.36 = bf16[4,4,256,512]{2,3,0,1:T(8,128)(2,1)} copy(bf16[4,4,256,512]{3,2,1,0:T(8,128)(2,1)} %pad_maximum_fusion) | data formatting | bytes 8388608 | tf_op jit(solution)/shard_map/stack | solution.py:189
  178.2 53.5 %all_to_all.10 = bf16[8,256,1024]{1,2,0:T(8,128)(2,1)} all-to-all(bf16[8,256,1024]{1,2,0:T(8,128)(2,1)} %bitcast.39), channel_id=1, replica_groups=mesh['seq'=8,'heads'=4] {'seq'}, dimensions={0} | all-to-all | bytes 8388608 | tf_op jit(solution)/shard_map/all_to_all | solution.py:191
  231.7 6.5 %copy.37 = bf16[8,256,1024]{2,1,0:T(8,128)(2,1)} copy(bf16[8,256,1024]{1,2,0:T(8,128)(2,1)} %all_to_all.10) | data formatting | bytes 8388608 | tf_op jit(solution)/shard_map/all_to_all | solution.py:191
  238.2 2.8 copy.38
  241.6 10.9 %convolution_convert_fusion = bf16[2048,2048]{1,0:T(8,128)(2,1)} fusion(bf16[2048,1024]{1,0:T(8,128)(2,1)S(1)} %bitcast.41, bf16[1024,2048]{1,0:T(8,128)(2,1)S(1)} %copy-done.10), kind=kOutput, calls=%fused_computation.1 | convolution fusion | flops 8594128896 | bytes 16777216 | tf_op jit(solution)/shard_map/dot_general | solution.py:195
  253.2 68.4 %reduce-scatter.2.cloned.1.call-done = bf16[256,2048]{1,0:T(8,128)(2,1)} async-done(((bf16[2048,2048]{1,0:T(8,128)(2,1)}), bf16[256,2048]{1,0:T(8,128)(2,1)}) %reduce-scatter.2.cloned.1.call-update) | async-done | bytes 1048592 | tf_op jit(solution)/shard_map/reduce_scatter | solution.py:194
  321.6 2.5 convolution_multiply_fusion
  326.4 11.7 %all-reduce = (f32[256]{0:T(256)S(1)}, f32[256]{0:T(256)S(1)}) all-reduce(f32[256]{0:T(256)S(1)} %get-tuple-element.5, f32[256]{0:T(256)S(1)} %get-tuple-element.4), channel_id=1, replica_groups=mesh['seq'=8,'heads'=4] {'heads'}, use_global_device_ids=true, to_apply=%region_8.9 | all-reduce | flops 512 | bytes 4096 | tf_op jit(solution)/shard_map/psum | solution.py:209
  338.1 3.1 fusion.2
  (52 shorter events, 8.4 us)
Async XLA Ops:
  7.2 1.2 copy-start
  9.7 7.0 %copy-start.9 = (s32[128]{0:T(128)S(1)}, s32[128]{0:T(128)}, u32[]{:S(2)}) copy-start(s32[128]{0:T(128)} %param.18) | copy-start | bytes 1540
  9.7 9.3 %copy-start.11 = (s32[8]{0:T(128)S(1)}, s32[8]{0:T(128)}, u32[]{:S(2)}) copy-start(s32[8]{0:T(128)} %param.16) | copy-start | bytes 100
  11.3 20.6 %all-to-all-start = ((bf16[8,2,16,2048]{3,2,1,0:T(8,128)(2,1)}), bf16[8,2,16,2048]{3,2,1,0:T(8,128)(2,1)S(1)}, u32[]{:S(2)}, u32[]{:S(2)}) async-start(bf16[8,2,16,2048]{3,2,1,0:T(8,128)(2,1)} %bitcast.5), calls=%async_computation | async-start | bytes 2097152 | tf_op jit(solution)/shard_map/all_to_all | solution.py:175
  16.5 91.0 %all-gather.9.cloned.1.call-start = ((), (), s32[]{:S(2)}) async-start(), calls=%async_computation.4 | async-start | bytes 1310720 | tf_op jit(solution)/shard_map/all_gather | solution.py:188
  31.9 2.9 copy-start.1
  50.6 57.4 %all-gather.11.cloned.1.call-start = ((), (), s32[]{:S(2)}) async-start(), calls=%async_computation.5 | async-start | bytes 1310720 | tf_op jit(solution)/shard_map/all_gather | solution.py:188
  50.7 2.9 copy-start.2
  69.5 68.2 %all-gather.13.cloned.1.call-start = ((), (), s32[]{:S(2)}) async-start(), calls=%async_computation.6 | async-start | bytes 1310720 | tf_op jit(solution)/shard_map/all_gather | solution.py:188
  69.5 2.9 copy-start.3
  88.3 78.8 %all-gather.15.cloned.1.call-start = ((), (), s32[]{:S(2)}) async-start(), calls=%async_computation.7 | async-start | bytes 1310720 | tf_op jit(solution)/shard_map/all_gather | solution.py:188
  88.4 2.9 copy-start.4
  107.2 214.5 %reduce-scatter.2.cloned.1.call-start = ((), (), s32[]{:S(2)}) async-start(), calls=%async_computation.3 | async-start | bytes 9437184 | tf_op jit(solution)/shard_map/reduce_scatter | solution.py:194
  238.2 3.4 copy-start.10
  324.1 1.3 copy-start.5
  324.1 1.5 copy-start.7
  324.1 1.5 copy-start.8
  326.3 14.9 %copy-start.6 = (bf16[256,2048]{1,0:T(8,128)(2,1)}, bf16[256,2048]{1,0:T(8,128)(2,1)S(1)}, u32[]{:S(2)}) copy-start(bf16[256,2048]{1,0:T(8,128)(2,1)S(1)} %get-tuple-element.8) | copy-start | bytes 3145732
Sparse Core Ops, SparseCore 0:
  50.8 28.2 all-gather.8
  80.6 27.4 all-gather.10
  110.2 27.4 all-gather.12
  139.7 27.4 all-gather.14
  252.7 68.9 reduce-scatter.1

commit v2 on v1

--- a/solution.py
+++ b/solution.py
@@ -1,3 +1,4 @@
+import functools
 import math
 
 import jax
@@ -122,13 +123,188 @@
             ],
         ),
         out_shape=jax.ShapeDtypeStruct((rows, width), jnp.bfloat16),
-        compiler_params=pltpu.CompilerParams(vmem_limit_bytes=40 * 2**20),
+        compiler_params=pltpu.CompilerParams(vmem_limit_bytes=60 * 2**20),
         cost_estimate=pl.CostEstimate(
             flops=4 * rows * width * keys,
             bytes_accessed=4 * keys * HEAD_DIM + 4 * rows * width,
             transcendentals=rows * width // HEAD_DIM * keys,
         ),
     )(order, first, tiles, flat, image_kv, image_kv)
+
+
+def project_body(seq_count, count, *refs):
+    parts = refs[:count]
+    w_ref, o_ref = refs[count : count + 2]
+    (held, stage, paired, summed, landed, own) = refs[count + 2 : count + 8]
+    (send_a, recv_a, send_p, recv_p, send_s, recv_s, local_sem) = refs[count + 8 :]
+    me = lax.axis_index("seq")
+    chips = seq_count // 2
+    chip, core = me // 2, lax.rem(me, 2)
+    sibling = chip * 2 + 1 - core
+    splits = count
+    rows, columns = own.shape
+    tile = 512
+    barrier = pltpu.get_barrier_semaphore()
+    for step in range(1, seq_count):
+        pl.semaphore_signal(
+            barrier,
+            inc=1,
+            device_id={"seq": lax.rem(me + step, seq_count)},
+            device_id_type=pl.DeviceIdType.MESH,
+        )
+    pl.semaphore_wait(barrier, seq_count - 1)
+
+    def context_copy(part, step):
+        target = lax.rem(me + step, seq_count)
+        return pltpu.make_async_remote_copy(
+            src_ref=parts[part].at[target // splits],
+            dst_ref=held.at[:, me],
+            send_sem=send_a.at[step],
+            recv_sem=recv_a.at[step],
+            device_id={"seq": target},
+            device_id_type=pl.DeviceIdType.MESH,
+        )
+
+    for step in list(range(2, seq_count)) + [1]:
+        for part in range(splits):
+            @pl.when(lax.rem(me + step, splits) == part)
+            def _():
+                context_copy(part, step).start()
+
+    for part in range(splits):
+        @pl.when(lax.rem(me, splits) == part)
+        def _():
+            kept = pltpu.make_async_copy(
+                parts[part].at[me // splits], held.at[:, me], local_sem
+            )
+            kept.start()
+            kept.wait()
+
+    for step in range(1, seq_count):
+        source = lax.rem(me + seq_count - step, seq_count)
+        pltpu.make_async_remote_copy(
+            src_ref=parts[0].at[0],
+            dst_ref=held.at[:, source],
+            send_sem=send_a.at[step],
+            recv_sem=recv_a.at[step],
+            device_id={"seq": source},
+            device_id_type=pl.DeviceIdType.MESH,
+        ).wait_recv()
+
+    def product(target, start):
+        left = held[target].reshape(rows, held.shape[3])
+        return jnp.dot(
+            left, w_ref[:, pl.ds(start, tile)], preferred_element_type=jnp.float32
+        )
+
+    def target_chip(step):
+        return lax.rem(chip + 1 + step, chips)
+
+    def pair_copy(step):
+        return pltpu.make_async_remote_copy(
+            src_ref=stage.at[step],
+            dst_ref=paired.at[step],
+            send_sem=send_p.at[step],
+            recv_sem=recv_p.at[step],
+            device_id={"seq": sibling},
+            device_id_type=pl.DeviceIdType.MESH,
+        )
+
+    def sum_copy(step):
+        return pltpu.make_async_remote_copy(
+            src_ref=summed.at[step],
+            dst_ref=landed.at[step],
+            send_sem=send_s.at[step],
+            recv_sem=recv_s.at[step],
+            device_id={"seq": target_chip(step) * 2 + core},
+            device_id_type=pl.DeviceIdType.MESH,
+        )
+
+    def give(step):
+        @pl.loop(0, columns // tile)
+        def _(index):
+            start = pl.multiple_of(index * tile, tile)
+            stage[step, :, pl.ds(start, tile)] = product(
+                target_chip(step) * 2 + 1 - core, start
+            ).astype(jnp.bfloat16)
+
+        pair_copy(step).start()
+
+    give(0)
+    for step in range(chips):
+        if step + 1 < chips:
+            give(step + 1)
+
+        @pl.loop(0, columns // tile)
+        def _(index):
+            start = pl.multiple_of(index * tile, tile)
+            own[:, pl.ds(start, tile)] = product(target_chip(step) * 2 + core, start)
+
+        pair_copy(step).wait_recv()
+        if step + 1 < chips:
+            @pl.loop(0, columns // tile)
+            def _(index):
+                span = pl.ds(pl.multiple_of(index * tile, tile), tile)
+                total = own[:, span] + paired[step, :, span].astype(jnp.float32)
+                summed[step, :, span] = total.astype(jnp.bfloat16)
+
+            sum_copy(step).start()
+
+    for step in range(chips - 1):
+        sum_copy(step).wait_recv()
+
+    @pl.loop(0, columns // tile)
+    def _(index):
+        span = pl.ds(pl.multiple_of(index * tile, tile), tile)
+        total = own[:, span] + paired[chips - 1, :, span].astype(jnp.float32)
+        for step in range(chips - 1):
+            total = total + landed[step, :, span].astype(jnp.float32)
+        o_ref[:, span] = total.astype(jnp.bfloat16)
+
+    for step in range(1, seq_count):
+        context_copy(0, step).wait_send()
+    for step in range(chips):
+        pair_copy(step).wait_send()
+    for step in range(chips - 1):
+        sum_copy(step).wait_send()
+
+
+def project_rows(parts, out_weight, seq_count):
+    count = len(parts)
+    depth, columns = out_weight.shape
+    piece = parts[0].shape[2]
+    rows = seq_count * piece
+    chips = seq_count // 2
+    return pl.pallas_call(
+        functools.partial(project_body, seq_count, count),
+        in_specs=[pl.BlockSpec(memory_space=pl.ANY)] * count
+        + [pl.BlockSpec(memory_space=pltpu.VMEM)],
+        out_specs=pl.BlockSpec(memory_space=pltpu.VMEM),
+        out_shape=jax.ShapeDtypeStruct((rows, columns), jnp.bfloat16),
+        scratch_shapes=[
+            pltpu.VMEM((seq_count, seq_count, piece, depth), jnp.bfloat16),
+            pltpu.VMEM((chips, rows, columns), jnp.bfloat16),
+            pltpu.VMEM((chips, rows, columns), jnp.bfloat16),
+            pltpu.VMEM((chips - 1, rows, columns), jnp.bfloat16),
+            pltpu.VMEM((chips - 1, rows, columns), jnp.bfloat16),
+            pltpu.VMEM((rows, columns), jnp.float32),
+            pltpu.SemaphoreType.DMA((seq_count,)),
+            pltpu.SemaphoreType.DMA((seq_count,)),
+            pltpu.SemaphoreType.DMA((chips,)),
+            pltpu.SemaphoreType.DMA((chips,)),
+            pltpu.SemaphoreType.DMA((chips,)),
+            pltpu.SemaphoreType.DMA((chips,)),
+            pltpu.SemaphoreType.DMA,
+        ],
+        compiler_params=pltpu.CompilerParams(
+            collective_id=0, has_side_effects=True, vmem_limit_bytes=56 * 2**20
+        ),
+        cost_estimate=pl.CostEstimate(
+            flops=2 * seq_count * rows * depth * columns,
+            bytes_accessed=2 * depth * columns + 2 * seq_count * rows * depth,
+            transcendentals=0,
+        ),
+    )(*parts, out_weight)
 
 
 def local(
@@ -178,25 +354,14 @@
     order = jnp.argsort(slot_first).astype(jnp.int32)
     sorted_first = slot_first[order]
     row_width = out_weight.shape[0]
-    width = group * HEAD_DIM // 2
-    pieces = row_width // width
-    gathered = []
+    width = min(group * HEAD_DIM, row_width)
+    parts = []
     for index in range(q_width // width):
-        mixed = attend(
-            order, sorted_first, tile_here[None], flat, image_kv, index, width, index // 2
-        )
-        gathered.append(lax.all_gather(mixed, "heads", axis=0))
-    stacked = jnp.stack(gathered).reshape(-1, pieces, len(gathered[0]), flat.shape[0], width)
-    outgoing = jnp.transpose(stacked, (2, 0, 3, 1, 4)).reshape(seq_count, flat.shape[0], row_width)
-    feature_rows = lax.all_to_all(outgoing, "seq", split_axis=0, concat_axis=0, tiled=True)
-    feature_rows = feature_rows.reshape(seq_count, seq_count, CAP * BLK, row_width)
-    feature_rows = jnp.swapaxes(feature_rows, 0, 1).reshape(-1, row_width)
-    slots = lax.psum_scatter(
-        jnp.dot(feature_rows, out_weight, preferred_element_type=jnp.float32).astype(jnp.bfloat16),
-        "seq",
-        scatter_dimension=0,
-        tiled=True,
-    )
+        kv_head = index * width // (group * HEAD_DIM)
+        mixed = attend(order, sorted_first, tile_here[None], flat, image_kv, index, width, kv_head)
+        gathered = lax.all_gather(mixed, "heads", axis=0)
+        parts.append(gathered.reshape(-1, seq_count, CAP * BLK, width))
+    slots = project_rows(parts, out_weight, seq_count)
     branch = jnp.einsum(
         "bs,src->brc",
         placing,

time: 349 us -> 286 us (0.82); the launches traced: 348 us -> 289 us
  Pallas kernels: 63.4 us -> 147 us
  blocking collectives: 65.2 us -> 9.51 us
  waiting for transfers between devices: 140 us -> 95.7 us
  local copies, waits for them, and re-layouts: 34.5 us -> 7.11 us
  matrix products: 14.7 us -> 3.81 us
  other arithmetic: 9.33 us -> 5.61 us
    pallas_call x0 -> x1, Pallas kernels: none -> 106 us  [project_rows(): pl.pallas_call(functools.partial(project_body, seq_count, count), in_spec...]
    reduce_scatter x1 -> x0, waiting for transfers between devices: 68.4 us -> none  [local(): lax.psum_scatter(jnp.dot(feature_rows, out_weight, preferred_element_type...]
    all_to_all x1 -> x0, blocking collectives: 53.5 us -> none  [local(): lax.all_to_all(outgoing, 'seq', split_axis=0, concat_axis=0, tiled=True)]
    all_gather x4 -> x2, waiting for transfers between devices: 59.7 us -> 84 us  [local(): gathered = lax.all_gather(mixed, 'heads', axis=0)]
    pallas_call x4 -> x2, Pallas kernels: 63.4 us -> 40.4 us  [attend(): pl.pallas_call(attend_body, grid_spec=pltpu.PrefetchScalarGridSpec(num_sc...]
    unnamed x24 -> x18, local copies, waits for them, and re-layouts: 12.7 us -> 1.49 us
    dot_general x1 -> x0, matrix products: 10.9 us -> none  [local(): jnp.dot(feature_rows, out_weight, preferred_element_type=jnp.float32)]
    another operation x1 -> x0, local copies, waits for them, and re-layouts: 7.3 us -> none  [local(): jnp.stack(gathered)]
  transfers between devices with their start and end apart: 6 -> 3, of which waited for: 5 -> 3; matrix products, arithmetic and copies ran while one was open for 1% -> 1% of each run, Pallas kernels for 14% -> 7%
where the time goes in v2:
time: 286 us; the launch traced here: 289 us
  Pallas kernels  147 us (51%)
  waiting for transfers between devices  95.7 us (33%)
  between operations  14.8 us (5%)
  blocking collectives  9.51 us (3%)
  local copies, waits for them, and re-layouts  7.11 us (2%)
  other arithmetic  5.61 us (2%)
  starting transfers between devices  5.43 us (2%)
  matrix products  3.81 us (1%)
    pallas_call x1, Pallas kernels, project_rows(): pl.pallas_call(functools.partial(project_body, seq_count, count), in_spec...  106 us
    all_gather x2, waiting for transfers between devices, local(): gathered = lax.all_gather(mixed, 'heads', axis=0)  84 us
    pallas_call x2, Pallas kernels, attend(): pl.pallas_call(attend_body, grid_spec=pltpu.PrefetchScalarGridSpec(num_sc...  40.4 us
    all_to_all x1, waiting for transfers between devices, local(): lax.all_to_all(outgoing, 'seq', split_axis=0, concat_axis=0, tiled=True)  11.7 us
    psum x1, blocking collectives, local(): lax.psum((jnp.sum(hidden * hidden, axis=1), jnp.sum(hidden * scaled, axis...  9.51 us
  transfers between devices with their start and end apart: 3, of which 3 were waited for; matrix products, arithmetic and copies ran while one was open for 1% of the time, Pallas kernels for 7%

profile of v2, /device:TPU:0, one launch (start us, length us, event | category | flops | bytes accessed | tf_op | source)
XLA Modules:
  0.0 288.7 jit_solution(7820812877215898318)
XLA Ops:
  7.2 0.8 reshape.66
  8.0 0.2 convert_reduce_fusion
  8.2 0.2 copy-done
  8.4 1.3 convolution_convert_fusion
  9.7 1.5 copy.30
  11.3 5.2 %all-to-all-start = ((bf16[8,2,16,2048]{3,2,1,0:T(8,128)(2,1)}), bf16[8,2,16,2048]{3,2,1,0:T(8,128)(2,1)S(1)}, u32[]{:S(2)}, u32[]{:S(2)}) async-start(bf16[8,2,16,2048]{3,2,1,0:T(8,128)(2,1)} %bitcast.5), calls=%async_computation | async-start | bytes 2097152 | tf_op jit(solution)/shard_map/all_to_all | solution.py:351
  16.5 0.2 reduce_window_sum.11
  17.1 1.3 sort.17
  18.4 1.2 gather_fusion
  19.6 0.6 dynamic_slice.9.tiles_ref
  20.2 11.7 %all-to-all-done = bf16[8,2,16,2048]{3,2,1,0:T(8,128)(2,1)S(1)} async-done(((bf16[8,2,16,2048]{3,2,1,0:T(8,128)(2,1)}), bf16[8,2,16,2048]{3,2,1,0:T(8,128)(2,1)S(1)}, u32[]{:S(2)}, u32[]{:S(2)}) %all-to-all-start) | async-done | bytes 1048608 | tf_op jit(solution)/shard_map/all_to_all | solution.py:351
  31.9 1.0 copy-done.4
  32.8 20.2 %shard_map.123 = bf16[256,1024]{1,0:T(8,128)(2,1)} custom-call(s32[16]{0:T(128)} %copy-done.8, s32[16]{0:T(128)} %gather_fusion, s32[1]{0:T(128)} %dynamic_slice.9.tiles_ref, bf16[256,2048]{1,0:T(8,128)(2,1)} %bitcast.22, bf16[1,2,6528,256]{3,2,1,0:T(8,128)(2,1)} %v_ref.3, bf16[1,2,6528,256]{3,2,1,0:T(8,128)(2,1)} %v_ref.3), custom_call_target="tpu_custom_call" | custom-call | flops 6845104128 | bytes 4390912 | tf_op jit(solution)/shard_map/pallas_call | solution.py:107
  53.1 0.2 all-gather.5.cloned.1.call-start
  53.3 20.2 %shard_map.122 = bf16[256,1024]{1,0:T(8,128)(2,1)} custom-call(s32[16]{0:T(128)} %copy-done.8, s32[16]{0:T(128)} %gather_fusion, s32[1]{0:T(128)} %dynamic_slice.9.tiles_ref, bf16[256,2048]{1,0:T(8,128)(2,1)} %bitcast.23, bf16[1,2,6528,256]{3,2,1,0:T(8,128)(2,1)} %v_ref.3, bf16[1,2,6528,256]{3,2,1,0:T(8,128)(2,1)} %v_ref.3), custom_call_target="tpu_custom_call" | custom-call | flops 6845104128 | bytes 4390912 | tf_op jit(solution)/shard_map/pallas_call | solution.py:107
  74.3 37.1 %all-gather.7.cloned.1.call-done = bf16[1024,1024]{1,0:T(8,128)(2,1)} async-done(((bf16[256,1024]{1,0:T(8,128)(2,1)}), bf16[1024,1024]{1,0:T(8,128)(2,1)}) %all-gather.7.cloned.1.call-update) | async-done | bytes 2097168 | tf_op jit(solution)/shard_map/all_gather | solution.py:362
  111.4 46.8 %all-gather.5.cloned.1.call-done = bf16[1024,1024]{1,0:T(8,128)(2,1)} async-done(((bf16[256,1024]{1,0:T(8,128)(2,1)}), bf16[1024,1024]{1,0:T(8,128)(2,1)}) %all-gather.5.cloned.1.call-update) | async-done | bytes 2097168 | tf_op jit(solution)/shard_map/all_gather | solution.py:362
  158.2 106.2 %shard_map.124 = bf16[256,2048]{1,0:T(8,128)(2,1)} custom-call(bf16[4,8,32,1024]{3,2,1,0:T(8,128)(2,1)} %bitcast.26, bf16[4,8,32,1024]{3,2,1,0:T(8,128)(2,1)} %bitcast.25, bf16[1024,2048]{1,0:T(8,128)(2,1)} %refs_2_.1), custom_call_target="tpu_custom_call" | custom-call | flops 8589934592 | bytes 8388608 | tf_op jit(solution)/shard_map/pallas_call | solution.py:278
  264.4 2.5 convolution_multiply_fusion
  267.0 1.2 copy.27
  268.2 0.3 copy-done.3
  268.5 0.7 fusion
  269.2 9.5 %all-reduce = (f32[256]{0:T(256)S(1)}, f32[256]{0:T(256)S(1)}) all-reduce(f32[256]{0:T(256)S(1)} %get-tuple-element.5, f32[256]{0:T(256)S(1)} %get-tuple-element.4), channel_id=1, replica_groups=mesh['seq'=8,'heads'=4] {'heads'}, use_global_device_ids=true, to_apply=%region_7.8 | all-reduce | flops 512 | bytes 4096 | tf_op jit(solution)/shard_map/psum | solution.py:374
  278.7 3.1 %fusion.2 = f32[256,2048]{1,0:T(8,128)} fusion(bf16[256,2048]{1,0:T(8,128)(2,1)S(1)} %get-tuple-element.8, bf16[256,2048]{1,0:T(8,128)(2,1)S(1)} %copy-done.1, bf16[256,2048]{1,0:T(8,128)(2,1)} %param.21, f32[256]{0:T(256)S(1)} %get-tuple-element.12, f32[2048]{0:T(1024)S(1)} %copy-done.5, f32[256]{0:T(256)S(1)} %get-tuple-element.11), kind=kLoop, calls=%fused_computation.8 | loop fusion | flops 4194304 | bytes 5253120 | tf_op jit(solution)/shard_map/sub | solution.py:380
  (30 shorter events, 0.6 us)
Async XLA Ops:
  7.2 1.2 copy-start
  9.7 7.0 %copy-start.6 = (s32[128]{0:T(128)S(1)}, s32[128]{0:T(128)}, u32[]{:S(2)}) copy-start(s32[128]{0:T(128)} %param.18) | copy-start | bytes 1540
  9.7 9.8 %copy-start.7 = (s32[8]{0:T(128)S(1)}, s32[8]{0:T(128)}, u32[]{:S(2)}) copy-start(s32[8]{0:T(128)} %param.16) | copy-start | bytes 100
  11.3 20.6 %all-to-all-start = ((bf16[8,2,16,2048]{3,2,1,0:T(8,128)(2,1)}), bf16[8,2,16,2048]{3,2,1,0:T(8,128)(2,1)S(1)}, u32[]{:S(2)}, u32[]{:S(2)}) async-start(bf16[8,2,16,2048]{3,2,1,0:T(8,128)(2,1)} %bitcast.5), calls=%async_computation | async-start | bytes 2097152 | tf_op jit(solution)/shard_map/all_to_all | solution.py:351
  16.5 94.9 %all-gather.7.cloned.1.call-start = ((), (), s32[]{:S(2)}) async-start(), calls=%async_computation.2 | async-start | bytes 2621440 | tf_op jit(solution)/shard_map/all_gather | solution.py:362
  18.4 13.5 %copy-start.8 = (s32[16]{0:T(128)}, s32[16]{0:T(128)S(1)}, u32[]{:S(2)}) copy-start(s32[16]{0:T(128)S(1)} %get-tuple-element.3.order_ref) | copy-start | bytes 196
  31.9 1.0 copy-start.4
  53.1 105.1 %all-gather.5.cloned.1.call-start = ((), (), s32[]{:S(2)}) async-start(), calls=%async_computation.1 | async-start | bytes 2621440 | tf_op jit(solution)/shard_map/all_gather | solution.py:362
  266.9 1.3 copy-start.1
  267.0 1.5 copy-start.3
  267.0 1.5 copy-start.5
  269.2 12.7 %copy-start.2 = (bf16[256,2048]{1,0:T(8,128)(2,1)}, bf16[256,2048]{1,0:T(8,128)(2,1)S(1)}, u32[]{:S(2)}) copy-start(bf16[256,2048]{1,0:T(8,128)(2,1)S(1)} %get-tuple-element.8) | copy-start | bytes 3145732
Sparse Core Ops, SparseCore 0:
  53.2 58.1 all-gather.6
  113.5 44.6 all-gather.4

commit v3 on v2

--- a/solution.py
+++ b/solution.py
@@ -135,8 +135,9 @@
 def project_body(seq_count, count, *refs):
     parts = refs[:count]
     w_ref, o_ref = refs[count : count + 2]
-    (held, stage, paired, summed, landed, own) = refs[count + 2 : count + 8]
-    (send_a, recv_a, send_p, recv_p, send_s, recv_s, local_sem) = refs[count + 8 :]
+    (held, stage, paired, summed, landed, own, gathered) = refs[count + 2 : count + 9]
+    (send_a, recv_a, send_p, recv_p, send_s, recv_s, local_sem, send_z, recv_z) = refs[count + 9 :]
+    plane, planes = lax.axis_index("heads"), gathered.shape[1]
     me = lax.axis_index("seq")
     chips = seq_count // 2
     chip, core = me // 2, lax.rem(me, 2)
@@ -152,41 +153,96 @@
             device_id={"seq": lax.rem(me + step, seq_count)},
             device_id_type=pl.DeviceIdType.MESH,
         )
-    pl.semaphore_wait(barrier, seq_count - 1)
-
-    def context_copy(part, step):
-        target = lax.rem(me + step, seq_count)
+    ways = (1, -1)
+
+    def inside(index):
+        return jnp.logical_and(index >= 0, index < planes)
+
+    for way in ways:
+        @pl.when(inside(plane + way))
+        def _():
+            pl.semaphore_signal(
+                barrier,
+                inc=1,
+                device_id={"heads": plane + way},
+                device_id_type=pl.DeviceIdType.MESH,
+            )
+
+    others = sum(inside(plane + way).astype(jnp.int32) for way in ways)
+    pl.semaphore_wait(barrier, seq_count - 1 + others)
+
+    def plane_copy(source, way, part, hop):
+        origin = plane - way * (hop - 1)
         return pltpu.make_async_remote_copy(
-            src_ref=parts[part].at[target // splits],
+            src_ref=source,
+            dst_ref=gathered.at[part, origin],
+            send_sem=send_z.at[max(way, 0), part, hop],
+            recv_sem=recv_z.at[max(way, 0), part, hop],
+            device_id={"heads": plane + way},
+            device_id_type=pl.DeviceIdType.MESH,
+        )
+
+    def context_copy(source, target):
+        return pltpu.make_async_remote_copy(
+            src_ref=source,
             dst_ref=held.at[:, me],
-            send_sem=send_a.at[step],
-            recv_sem=recv_a.at[step],
+            send_sem=send_a.at[target],
+            recv_sem=recv_a.at[me],
             device_id={"seq": target},
             device_id_type=pl.DeviceIdType.MESH,
         )
 
-    for step in list(range(2, seq_count)) + [1]:
-        for part in range(splits):
-            @pl.when(lax.rem(me + step, splits) == part)
-            def _():
-                context_copy(part, step).start()
-
-    for part in range(splits):
-        @pl.when(lax.rem(me, splits) == part)
+    def deliver(source, target):
+        @pl.when(target != me)
         def _():
-            kept = pltpu.make_async_copy(
-                parts[part].at[me // splits], held.at[:, me], local_sem
-            )
+            context_copy(source, target).start()
+
+        @pl.when(target == me)
+        def _():
+            kept = pltpu.make_async_copy(source, held.at[:, me], local_sem)
             kept.start()
             kept.wait()
+
+    for part in range(splits):
+        for way in ways:
+            @pl.when(inside(plane + way))
+            def _():
+                plane_copy(parts[part], way, part, 1).start()
+
+    for part in range(splits):
+        deliver(parts[part], plane * splits + part)
+
+    for hop in range(1, planes):
+        for part in range(splits):
+            for way in ways:
+                origin = plane - way * hop
+
+                @pl.when(inside(origin))
+                def _():
+                    block = gathered.at[part, origin]
+                    pltpu.make_async_remote_copy(
+                        src_ref=block,
+                        dst_ref=block,
+                        send_sem=send_z.at[max(way, 0), part, hop],
+                        recv_sem=recv_z.at[max(way, 0), part, hop],
+                        device_id={"heads": plane - way},
+                        device_id_type=pl.DeviceIdType.MESH,
+                    ).wait_recv()
+
+                    if hop + 1 < planes:
+                        @pl.when(inside(plane + way))
+                        def _():
+                            plane_copy(block, way, part, hop + 1).start()
+
+                    deliver(block, origin * splits + part)
 
     for step in range(1, seq_count):
         source = lax.rem(me + seq_count - step, seq_count)
         pltpu.make_async_remote_copy(
-            src_ref=parts[0].at[0],
+            src_ref=parts[0],
             dst_ref=held.at[:, source],
-            send_sem=send_a.at[step],
-            recv_sem=recv_a.at[step],
+            send_sem=send_a.at[source],
+            recv_sem=recv_a.at[source],
             device_id={"seq": source},
             device_id_type=pl.DeviceIdType.MESH,
         ).wait_recv()
@@ -262,7 +318,15 @@
         o_ref[:, span] = total.astype(jnp.bfloat16)
 
     for step in range(1, seq_count):
-        context_copy(0, step).wait_send()
+        context_copy(parts[0], lax.rem(me + step, seq_count)).wait_send()
+    for hop in range(1, planes):
+        for part in range(splits):
+            for way in ways:
+                sent = jnp.logical_and(inside(plane - way * (hop - 1)), inside(plane + way))
+
+                @pl.when(sent)
+                def _():
+                    plane_copy(parts[part], way, part, hop).wait_send()
     for step in range(chips):
         pair_copy(step).wait_send()
     for step in range(chips - 1):
@@ -272,7 +336,8 @@
 def project_rows(parts, out_weight, seq_count):
     count = len(parts)
     depth, columns = out_weight.shape
-    piece = parts[0].shape[2]
+    piece = parts[0].shape[1]
+    planes = lax.axis_size("heads")
     rows = seq_count * piece
     chips = seq_count // 2
     return pl.pallas_call(
@@ -288,6 +353,7 @@
             pltpu.VMEM((chips - 1, rows, columns), jnp.bfloat16),
             pltpu.VMEM((chips - 1, rows, columns), jnp.bfloat16),
             pltpu.VMEM((rows, columns), jnp.float32),
+            pltpu.VMEM((count, planes, seq_count, piece, depth), jnp.bfloat16),
             pltpu.SemaphoreType.DMA((seq_count,)),
             pltpu.SemaphoreType.DMA((seq_count,)),
             pltpu.SemaphoreType.DMA((chips,)),
@@ -295,6 +361,8 @@
             pltpu.SemaphoreType.DMA((chips,)),
             pltpu.SemaphoreType.DMA((chips,)),
             pltpu.SemaphoreType.DMA,
+            pltpu.SemaphoreType.DMA((2, count, planes)),
+            pltpu.SemaphoreType.DMA((2, count, planes)),
         ],
         compiler_params=pltpu.CompilerParams(
             collective_id=0, has_side_effects=True, vmem_limit_bytes=56 * 2**20
@@ -359,8 +427,7 @@
     for index in range(q_width // width):
         kv_head = index * width // (group * HEAD_DIM)
         mixed = attend(order, sorted_first, tile_here[None], flat, image_kv, index, width, kv_head)
-        gathered = lax.all_gather(mixed, "heads", axis=0)
-        parts.append(gathered.reshape(-1, seq_count, CAP * BLK, width))
+        parts.append(mixed.reshape(seq_count, CAP * BLK, width))
     slots = project_rows(parts, out_weight, seq_count)
     branch = jnp.einsum(
         "bs,src->brc",

time: 286 us -> 288 us (level)
  waiting for transfers between devices: 95.7 us -> 11.1 us
  Pallas kernels: 147 us -> 226 us
  blocking collectives: 9.51 us -> 29.1 us
  between operations: 14.8 us -> 1.43 us
    pallas_call x1, Pallas kernels: 106 us -> 198 us  [project_rows(): pl.pallas_call(functools.partial(project_body, seq_count, count), in_spec...]
    all_gather x2 -> x0, waiting for transfers between devices: 84 us -> none  [local(): gathered = lax.all_gather(mixed, 'heads', axis=0)]
    psum x1, blocking collectives: 9.51 us -> 29.1 us  [local(): lax.psum((jnp.sum(hidden * hidden, axis=1), jnp.sum(hidden * scaled, axis...]
    pallas_call x2, Pallas kernels: 40.4 us -> 27.7 us  [attend(): pl.pallas_call(attend_body, grid_spec=pltpu.PrefetchScalarGridSpec(num_sc...]
  transfers between devices with their start and end apart: 3 -> 1, of which waited for: 3 -> 1; matrix products, arithmetic and copies ran while one was open for 1% -> 1% of each run, Pallas kernels for 7% -> 0%
where the time goes in v3:
time: 288 us; the launch traced here: 289 us
  Pallas kernels  226 us (78%)
  blocking collectives  29.1 us (10%)
  waiting for transfers between devices  11.1 us (4%)
  local copies, waits for them, and re-layouts  7.1 us (2%)
  other arithmetic  5.61 us (2%)
  starting transfers between devices  5.17 us (2%)
  matrix products  3.81 us (1%)
    pallas_call x1, Pallas kernels, project_rows(): pl.pallas_call(functools.partial(project_body, seq_count, count), in_spec...  198 us
    psum x1, blocking collectives, local(): lax.psum((jnp.sum(hidden * hidden, axis=1), jnp.sum(hidden * scaled, axis...  29.1 us
    pallas_call x2, Pallas kernels, attend(): pl.pallas_call(attend_body, grid_spec=pltpu.PrefetchScalarGridSpec(num_sc...  27.7 us
    all_to_all x1, waiting for transfers between devices, local(): lax.all_to_all(outgoing, 'seq', split_axis=0, concat_axis=0, tiled=True)  11.1 us
  transfers between devices with their start and end apart: 1, of which 1 were waited for; matrix products, arithmetic and copies ran while one was open for 1% of the time, Pallas kernels for 0%

profile of v3, /device:TPU:0, one launch (start us, length us, event | category | flops | bytes accessed | tf_op | source)
XLA Modules:
  0.0 288.9 jit_solution(2099145546713524622)
XLA Ops:
  0.6 0.8 reshape.66
  1.5 0.2 convert_reduce_fusion
  1.7 0.2 copy-done
  1.9 1.3 convolution_convert_fusion
  3.2 1.5 copy.30
  4.8 5.2 %all-to-all-start = ((bf16[8,2,16,2048]{3,2,1,0:T(8,128)(2,1)}), bf16[8,2,16,2048]{3,2,1,0:T(8,128)(2,1)S(1)}, u32[]{:S(2)}, u32[]{:S(2)}) async-start(bf16[8,2,16,2048]{3,2,1,0:T(8,128)(2,1)} %bitcast.5), calls=%async_computation | async-start | bytes 2097152 | tf_op jit(solution)/shard_map/all_to_all | solution.py:419
  10.6 0.6 dynamic_slice.9.tiles_ref
  11.3 0.2 reduce_window_sum.11
  11.5 0.1 select_reduce_fusion
  11.7 0.1 copy.22
  11.7 0.1 reshape.67
  11.8 1.3 sort.17
  13.1 1.2 gather_fusion
  14.3 11.1 %all-to-all-done = bf16[8,2,16,2048]{3,2,1,0:T(8,128)(2,1)S(1)} async-done(((bf16[8,2,16,2048]{3,2,1,0:T(8,128)(2,1)}), bf16[8,2,16,2048]{3,2,1,0:T(8,128)(2,1)S(1)}, u32[]{:S(2)}, u32[]{:S(2)}) %all-to-all-start) | async-done | bytes 1048608 | tf_op jit(solution)/shard_map/all_to_all | solution.py:419
  25.3 1.0 copy-done.4
  26.3 13.8 %shard_map.123 = bf16[256,1024]{1,0:T(8,128)(2,1)} custom-call(s32[16]{0:T(128)} %copy-done.8, s32[16]{0:T(128)} %gather_fusion, s32[1]{0:T(128)} %dynamic_slice.9.tiles_ref, bf16[256,2048]{1,0:T(8,128)(2,1)} %bitcast.22, bf16[1,2,6528,256]{3,2,1,0:T(8,128)(2,1)} %v_ref.3, bf16[1,2,6528,256]{3,2,1,0:T(8,128)(2,1)} %v_ref.3), custom_call_target="tpu_custom_call" | custom-call | flops 6845104128 | bytes 4390912 | tf_op jit(solution)/shard_map/pallas_call | solution.py:107
  40.1 13.8 %shard_map.122 = bf16[256,1024]{1,0:T(8,128)(2,1)} custom-call(s32[16]{0:T(128)} %copy-done.8, s32[16]{0:T(128)} %gather_fusion, s32[1]{0:T(128)} %dynamic_slice.9.tiles_ref, bf16[256,2048]{1,0:T(8,128)(2,1)} %bitcast.23, bf16[1,2,6528,256]{3,2,1,0:T(8,128)(2,1)} %v_ref.3, bf16[1,2,6528,256]{3,2,1,0:T(8,128)(2,1)} %v_ref.3), custom_call_target="tpu_custom_call" | custom-call | flops 6845104128 | bytes 4390912 | tf_op jit(solution)/shard_map/pallas_call | solution.py:107
  54.0 198.0 %shard_map.124 = bf16[256,2048]{1,0:T(8,128)(2,1)} custom-call(bf16[8,32,1024]{2,1,0:T(8,128)(2,1)} %bitcast.26, bf16[8,32,1024]{2,1,0:T(8,128)(2,1)} %bitcast.25, bf16[1024,2048]{1,0:T(8,128)(2,1)} %refs_2_.1), custom_call_target="tpu_custom_call" | custom-call | flops 8589934592 | bytes 8388608 | tf_op jit(solution)/shard_map/pallas_call | solution.py:343
  252.0 2.5 convolution_multiply_fusion
  254.5 1.2 copy.27
  255.7 0.3 copy-done.3
  256.0 0.7 fusion
  256.7 29.1 %all-reduce = (f32[256]{0:T(256)S(1)}, f32[256]{0:T(256)S(1)}) all-reduce(f32[256]{0:T(256)S(1)} %get-tuple-element.5, f32[256]{0:T(256)S(1)} %get-tuple-element.4), channel_id=1, replica_groups=mesh['seq'=8,'heads'=4] {'heads'}, use_global_device_ids=true, to_apply=%region_7.8 | all-reduce | flops 512 | bytes 4096 | tf_op jit(solution)/shard_map/psum | solution.py:441
  285.8 3.1 %fusion.2 = f32[256,2048]{1,0:T(8,128)} fusion(bf16[256,2048]{1,0:T(8,128)(2,1)S(1)} %get-tuple-element.8, bf16[256,2048]{1,0:T(8,128)(2,1)S(1)} %copy-done.1, bf16[256,2048]{1,0:T(8,128)(2,1)} %param.21, f32[256]{0:T(256)S(1)} %get-tuple-element.12, f32[2048]{0:T(1024)S(1)} %copy-done.5, f32[256]{0:T(256)S(1)} %get-tuple-element.11), kind=kLoop, calls=%fused_computation.8 | loop fusion | flops 4194304 | bytes 5253120 | tf_op jit(solution)/shard_map/sub | solution.py:447
  (24 shorter events, 0.2 us)
Async XLA Ops:
  0.6 1.2 copy-start
  3.2 7.4 %copy-start.7 = (s32[8]{0:T(128)S(1)}, s32[8]{0:T(128)}, u32[]{:S(2)}) copy-start(s32[8]{0:T(128)} %param.16) | copy-start | bytes 100
  3.2 8.2 %copy-start.6 = (s32[128]{0:T(128)S(1)}, s32[128]{0:T(128)}, u32[]{:S(2)}) copy-start(s32[128]{0:T(128)} %param.18) | copy-start | bytes 1540
  4.8 20.6 %all-to-all-start = ((bf16[8,2,16,2048]{3,2,1,0:T(8,128)(2,1)}), bf16[8,2,16,2048]{3,2,1,0:T(8,128)(2,1)S(1)}, u32[]{:S(2)}, u32[]{:S(2)}) async-start(bf16[8,2,16,2048]{3,2,1,0:T(8,128)(2,1)} %bitcast.5), calls=%async_computation | async-start | bytes 2097152 | tf_op jit(solution)/shard_map/all_to_all | solution.py:419
  13.1 12.3 %copy-start.8 = (s32[16]{0:T(128)}, s32[16]{0:T(128)S(1)}, u32[]{:S(2)}) copy-start(s32[16]{0:T(128)S(1)} %get-tuple-element.3.order_ref) | copy-start | bytes 196
  25.3 1.0 copy-start.4
  254.5 1.3 copy-start.1
  254.5 1.5 copy-start.3
  254.5 1.5 copy-start.5
  256.7 32.2 %copy-start.2 = (bf16[256,2048]{1,0:T(8,128)(2,1)}, bf16[256,2048]{1,0:T(8,128)(2,1)S(1)}, u32[]{:S(2)}) copy-start(bf16[256,2048]{1,0:T(8,128)(2,1)S(1)} %get-tuple-element.8) | copy-start | bytes 3145732

commit v4 on v3

--- a/solution.py
+++ b/solution.py
@@ -203,17 +203,20 @@
             kept.start()
             kept.wait()
 
-    for part in range(splits):
+    for part in range(1, splits):
         for way in ways:
             @pl.when(inside(plane + way))
             def _():
                 plane_copy(parts[part], way, part, 1).start()
 
-    for part in range(splits):
+    for shift in range(planes):
+        first = lax.rem(plane + shift, planes)
+        deliver(parts[0].at[first], first * splits)
+    for part in range(1, splits):
         deliver(parts[part], plane * splits + part)
 
     for hop in range(1, planes):
-        for part in range(splits):
+        for part in range(1, splits):
             for way in ways:
                 origin = plane - way * hop
 
@@ -239,7 +242,7 @@
     for step in range(1, seq_count):
         source = lax.rem(me + seq_count - step, seq_count)
         pltpu.make_async_remote_copy(
-            src_ref=parts[0],
+            src_ref=parts[-1],
             dst_ref=held.at[:, source],
             send_sem=send_a.at[source],
             recv_sem=recv_a.at[source],
@@ -318,9 +321,9 @@
         o_ref[:, span] = total.astype(jnp.bfloat16)
 
     for step in range(1, seq_count):
-        context_copy(parts[0], lax.rem(me + step, seq_count)).wait_send()
+        context_copy(parts[-1], lax.rem(me + step, seq_count)).wait_send()
     for hop in range(1, planes):
-        for part in range(splits):
+        for part in range(1, splits):
             for way in ways:
                 sent = jnp.logical_and(inside(plane - way * (hop - 1)), inside(plane + way))
 
@@ -336,7 +339,7 @@
 def project_rows(parts, out_weight, seq_count):
     count = len(parts)
     depth, columns = out_weight.shape
-    piece = parts[0].shape[1]
+    piece = parts[-1].shape[1]
     planes = lax.axis_size("heads")
     rows = seq_count * piece
     chips = seq_count // 2
@@ -427,7 +430,11 @@
     for index in range(q_width // width):
         kv_head = index * width // (group * HEAD_DIM)
         mixed = attend(order, sorted_first, tile_here[None], flat, image_kv, index, width, kv_head)
-        parts.append(mixed.reshape(seq_count, CAP * BLK, width))
+        if index == 0:
+            mixed = lax.all_gather(mixed, "heads", axis=0)
+            parts.append(mixed.reshape(-1, seq_count, CAP * BLK, width))
+        else:
+            parts.append(mixed.reshape(seq_count, CAP * BLK, width))
     slots = project_rows(parts, out_weight, seq_count)
     branch = jnp.einsum(
         "bs,src->brc",

time: 288 us -> 274 us (0.951); the launches traced: 289 us -> 271 us
  Pallas kernels: 226 us -> 160 us
  waiting for transfers between devices: 11.1 us -> 36.3 us
  between operations: 1.43 us -> 14.8 us
  blocking collectives: 29.1 us -> 38.2 us
    pallas_call x1, Pallas kernels: 198 us -> 111 us  [project_rows(): pl.pallas_call(functools.partial(project_body, seq_count, count), in_spec...]
    all_gather x0 -> x1, waiting for transfers between devices: none -> 24.6 us  [local(): mixed = lax.all_gather(mixed, 'heads', axis=0)]
    pallas_call x2, Pallas kernels: 27.7 us -> 49 us  [attend(): pl.pallas_call(attend_body, grid_spec=pltpu.PrefetchScalarGridSpec(num_sc...]
    psum x1, blocking collectives: 29.1 us -> 38.2 us  [local(): lax.psum((jnp.sum(hidden * hidden, axis=1), jnp.sum(hidden * scaled, axis...]
  transfers between devices with their start and end apart: 1 -> 2, of which waited for: 1 -> 2; matrix products, arithmetic and copies ran while one was open for 1% -> 1% of each run, Pallas kernels for 0% -> 9%
where the time goes in v4:
time: 274 us; the launch traced here: 271 us
  Pallas kernels  160 us (58%)
  blocking collectives  38.2 us (14%)
  waiting for transfers between devices  36.3 us (13%)
  between operations  14.8 us (5%)
  local copies, waits for them, and re-layouts  7.12 us (3%)
  other arithmetic  5.61 us (2%)
  starting transfers between devices  5.21 us (2%)
  matrix products  3.81 us (1%)
    pallas_call x1, Pallas kernels, project_rows(): pl.pallas_call(functools.partial(project_body, seq_count, count), in_spec...  111 us
    pallas_call x2, Pallas kernels, attend(): pl.pallas_call(attend_body, grid_spec=pltpu.PrefetchScalarGridSpec(num_sc...  49 us
    psum x1, blocking collectives, local(): lax.psum((jnp.sum(hidden * hidden, axis=1), jnp.sum(hidden * scaled, axis...  38.2 us
    all_gather x1, waiting for transfers between devices, local(): mixed = lax.all_gather(mixed, 'heads', axis=0)  24.6 us
    all_to_all x1, waiting for transfers between devices, local(): lax.all_to_all(outgoing, 'seq', split_axis=0, concat_axis=0, tiled=True)  11.7 us
  transfers between devices with their start and end apart: 2, of which 2 were waited for; matrix products, arithmetic and copies ran while one was open for 1% of the time, Pallas kernels for 9%

profile of v4, /device:TPU:0, one launch (start us, length us, event | category | flops | bytes accessed | tf_op | source)
XLA Modules:
  0.0 271.1 jit_solution(15484395719662875954)
XLA Ops:
  7.2 0.8 reshape.66
  8.0 0.2 convert_reduce_fusion
  8.2 0.2 copy-done
  8.4 1.3 convolution_convert_fusion
  9.7 1.5 copy.30
  11.3 5.2 %all-to-all-start = ((bf16[8,2,16,2048]{3,2,1,0:T(8,128)(2,1)}), bf16[8,2,16,2048]{3,2,1,0:T(8,128)(2,1)S(1)}, u32[]{:S(2)}, u32[]{:S(2)}) async-start(bf16[8,2,16,2048]{3,2,1,0:T(8,128)(2,1)} %bitcast.5), calls=%async_computation | async-start | bytes 2097152 | tf_op jit(solution)/shard_map/all_to_all | solution.py:422
  16.5 0.6 dynamic_slice.9.tiles_ref
  17.1 0.2 reduce_window_sum.11
  17.4 0.1 select_reduce_fusion
  17.5 0.1 copy.22
  17.7 1.3 sort.17
  19.0 1.2 gather_fusion
  20.2 11.7 %all-to-all-done = bf16[8,2,16,2048]{3,2,1,0:T(8,128)(2,1)S(1)} async-done(((bf16[8,2,16,2048]{3,2,1,0:T(8,128)(2,1)}), bf16[8,2,16,2048]{3,2,1,0:T(8,128)(2,1)S(1)}, u32[]{:S(2)}, u32[]{:S(2)}) %all-to-all-start) | async-done | bytes 1048608 | tf_op jit(solution)/shard_map/all_to_all | solution.py:422
  31.9 1.0 copy-done.4
  32.8 24.5 %shard_map.122 = bf16[256,1024]{1,0:T(8,128)(2,1)} custom-call(s32[16]{0:T(128)} %copy-done.8, s32[16]{0:T(128)} %gather_fusion, s32[1]{0:T(128)} %dynamic_slice.9.tiles_ref, bf16[256,2048]{1,0:T(8,128)(2,1)} %bitcast.22, bf16[1,2,6528,256]{3,2,1,0:T(8,128)(2,1)} %v_ref.3, bf16[1,2,6528,256]{3,2,1,0:T(8,128)(2,1)} %v_ref.3), custom_call_target="tpu_custom_call" | custom-call | flops 6845104128 | bytes 4390912 | tf_op jit(solution)/shard_map/pallas_call | solution.py:107
  58.1 24.5 %shard_map.123 = bf16[256,1024]{1,0:T(8,128)(2,1)} custom-call(s32[16]{0:T(128)} %copy-done.8, s32[16]{0:T(128)} %gather_fusion, s32[1]{0:T(128)} %dynamic_slice.9.tiles_ref, bf16[256,2048]{1,0:T(8,128)(2,1)} %bitcast.23, bf16[1,2,6528,256]{3,2,1,0:T(8,128)(2,1)} %v_ref.3, bf16[1,2,6528,256]{3,2,1,0:T(8,128)(2,1)} %v_ref.3), custom_call_target="tpu_custom_call" | custom-call | flops 6845104128 | bytes 4390912 | tf_op jit(solution)/shard_map/pallas_call | solution.py:107
  82.6 24.6 %all-gather.3.cloned.1.call-done = bf16[1024,1024]{1,0:T(8,128)(2,1)} async-done(((bf16[256,1024]{1,0:T(8,128)(2,1)}), bf16[1024,1024]{1,0:T(8,128)(2,1)}) %all-gather.3.cloned.1.call-update) | async-done | bytes 2097168 | tf_op jit(solution)/shard_map/all_gather | solution.py:434
  107.1 111.0 %shard_map.124 = bf16[256,2048]{1,0:T(8,128)(2,1)} custom-call(bf16[4,8,32,1024]{3,2,1,0:T(8,128)(2,1)} %bitcast.25, bf16[8,32,1024]{2,1,0:T(8,128)(2,1)} %bitcast.26, bf16[1024,2048]{1,0:T(8,128)(2,1)} %refs_2_.1), custom_call_target="tpu_custom_call" | custom-call | flops 8589934592 | bytes 8388608 | tf_op jit(solution)/shard_map/pallas_call | solution.py:346
  218.2 2.5 convolution_multiply_fusion
  220.7 1.2 copy.27
  221.9 0.3 copy-done.3
  222.2 0.7 fusion
  222.9 38.2 %all-reduce = (f32[256]{0:T(256)S(1)}, f32[256]{0:T(256)S(1)}) all-reduce(f32[256]{0:T(256)S(1)} %get-tuple-element.5, f32[256]{0:T(256)S(1)} %get-tuple-element.4), channel_id=1, replica_groups=mesh['seq'=8,'heads'=4] {'heads'}, use_global_device_ids=true, to_apply=%region_7.8 | all-reduce | flops 512 | bytes 4096 | tf_op jit(solution)/shard_map/psum | solution.py:448
  261.1 3.1 %fusion.2 = f32[256,2048]{1,0:T(8,128)} fusion(bf16[256,2048]{1,0:T(8,128)(2,1)S(1)} %get-tuple-element.8, bf16[256,2048]{1,0:T(8,128)(2,1)S(1)} %copy-done.1, bf16[256,2048]{1,0:T(8,128)(2,1)} %param.21, f32[256]{0:T(256)S(1)} %get-tuple-element.12, f32[2048]{0:T(1024)S(1)} %copy-done.5, f32[256]{0:T(256)S(1)} %get-tuple-element.11), kind=kLoop, calls=%fused_computation.8 | loop fusion | flops 4194304 | bytes 5253120 | tf_op jit(solution)/shard_map/sub | solution.py:454
  (27 shorter events, 0.3 us)
Async XLA Ops:
  7.2 1.2 copy-start
  9.7 6.8 %copy-start.7 = (s32[8]{0:T(128)S(1)}, s32[8]{0:T(128)}, u32[]{:S(2)}) copy-start(s32[8]{0:T(128)} %param.16) | copy-start | bytes 100
  9.7 7.6 %copy-start.6 = (s32[128]{0:T(128)S(1)}, s32[128]{0:T(128)}, u32[]{:S(2)}) copy-start(s32[128]{0:T(128)} %param.18) | copy-start | bytes 1540
  11.3 20.6 %all-to-all-start = ((bf16[8,2,16,2048]{3,2,1,0:T(8,128)(2,1)}), bf16[8,2,16,2048]{3,2,1,0:T(8,128)(2,1)S(1)}, u32[]{:S(2)}, u32[]{:S(2)}) async-start(bf16[8,2,16,2048]{3,2,1,0:T(8,128)(2,1)} %bitcast.5), calls=%async_computation | async-start | bytes 2097152 | tf_op jit(solution)/shard_map/all_to_all | solution.py:422
  16.5 90.7 %all-gather.3.cloned.1.call-start = ((), (), s32[]{:S(2)}) async-start(), calls=%async_computation.1 | async-start | bytes 2621440 | tf_op jit(solution)/shard_map/all_gather | solution.py:434
  19.0 12.9 %copy-start.8 = (s32[16]{0:T(128)}, s32[16]{0:T(128)S(1)}, u32[]{:S(2)}) copy-start(s32[16]{0:T(128)S(1)} %get-tuple-element.3.order_ref) | copy-start | bytes 196
  31.9 1.0 copy-start.4
  220.7 1.3 copy-start.1
  220.7 1.5 copy-start.3
  220.7 1.5 copy-start.5
  222.9 41.4 %copy-start.2 = (bf16[256,2048]{1,0:T(8,128)(2,1)}, bf16[256,2048]{1,0:T(8,128)(2,1)S(1)}, u32[]{:S(2)}) copy-start(bf16[256,2048]{1,0:T(8,128)(2,1)S(1)} %get-tuple-element.8) | copy-start | bytes 3145732
Sparse Core Ops, SparseCore 0:
  57.5 49.6 all-gather.2
